TPU v7x, 32 devices: a whole 2x2x4 slice. The times are simulated.
32 devices in a mesh: row: 4 (over y, x), blk: 8 (over z, core).
Axes of the slice: x: 2, y: 2, z: 4, core: 2. Of those that a mesh axis runs over, the one named last changes fastest.
Arguments:
- grad: bfloat16 [4, 1024, 4096], P(None, 'row', 'blk'), may hold values from -6 to 6
- exp_avg: float32 [4, 1024, 4096], P(None, 'row', 'blk'), may hold values from -6 to 6
- exp_avg_sq: float32 [4, 1024, 4096], P(None, 'row', 'blk'), may hold values from 0.1 to 4
- left_basis: bfloat16 [4, 1024, 1024], P(None, 'row', 'blk'), may hold values from -0.1875 to 0.1875
- right_basis: bfloat16 [4096, 1024], P('blk', 'row'), may hold values from -0.1875 to 0.1875
Outputs:
- update: bfloat16 [4, 1024, 4096], P(None, 'row', 'blk')
- moment: float32 [4, 1024, 4096], P(None, 'row', 'blk')
- variance: float32 [4, 1024, 4096], P(None, 'row', 'blk')
All inputs are finite; a program needn't handle non-finite values.
Results may differ from a plain program's by a relative error of at most 0.0061.
Values may be sent and summed in bfloat16 or wider, within the bound.
A program may use at most 128 MiB of HBM per device.

v0:
```python
import jax
import jax.numpy as jnp
from jax import lax
from jax.sharding import PartitionSpec as P

momentum_decay = 0.9
variance_decay = 0.95
epsilon_value = 1e-08


def from_partner(value, axis, bit):
    mask = 2**bit
    pairs = [(source, source ^ mask) for source in range(lax.axis_size(axis))]
    return lax.ppermute(value, axis, pairs)


def spread_block(data, groups):
    blocks, brows, cols = data.shape
    narrow = cols // groups
    return (
        data.reshape(blocks, brows, groups, narrow)
        .transpose(0, 2, 1, 3)
        .reshape(blocks * groups, brows, narrow)
    )


def join_block(data, blocks, groups):
    total, brows, narrow = data.shape
    return (
        data.reshape(blocks, groups, brows, narrow)
        .transpose(0, 2, 1, 3)
        .reshape(blocks, brows, groups * narrow)
    )


def body(grad, exp_avg, exp_avg_sq, left_basis, right_basis):
    blocks, brows, cols = grad.shape
    moment = momentum_decay * exp_avg + (1.0 - momentum_decay) * grad.astype(jnp.float32)
    moment_half = moment.astype(jnp.bfloat16)
    left_rows = lax.all_gather(left_basis, "blk", axis=2, tiled=True)
    right_rows = lax.all_gather(right_basis, "row", axis=1, tiled=True)
    groups = lax.axis_size("row") // blocks
    grad_group, moment_group = (
        lax.all_to_all(spread_block(grad, groups), "row", split_axis=0, concat_axis=1, tiled=True),
        lax.all_to_all(
            spread_block(moment_half, groups), "row", split_axis=0, concat_axis=1, tiled=True
        ),
    )
    picked = jnp.repeat(left_rows, groups, axis=0)
    block_rows = lax.all_to_all(picked, "row", split_axis=0, concat_axis=0, tiled=True)
    own_block = block_rows.reshape(block_rows.shape[0] * brows, block_rows.shape[2])
    grad_turned = jnp.einsum(
        "kn,kc->nc", own_block, grad_group[0], preferred_element_type=jnp.float32
    ).astype(jnp.bfloat16)
    moment_turned = jnp.einsum(
        "kn,kc->nc", own_block, moment_group[0], preferred_element_type=jnp.float32
    ).astype(jnp.bfloat16)
    grad_back, moment_back = (
        lax.all_to_all(grad_turned[None], "row", split_axis=1, concat_axis=0, tiled=True),
        lax.all_to_all(moment_turned[None], "row", split_axis=1, concat_axis=0, tiled=True),
    )
    grad_left = join_block(grad_back, blocks, groups)
    moment_left = join_block(moment_back, blocks, groups)
    half = lax.axis_index("blk") % 2
    grad_term = jnp.dot(
        grad_left.reshape(blocks * brows, cols), right_rows, preferred_element_type=jnp.float32
    )
    moment_term = jnp.dot(
        moment_left.reshape(blocks * brows, cols), right_rows, preferred_element_type=jnp.float32
    )
    own_start = half * cols
    other_start = (1 - half) * cols
    grad_other, moment_other = from_partner(
        (
            lax.dynamic_slice_in_dim(grad_term, other_start, cols, 1),
            lax.dynamic_slice_in_dim(moment_term, other_start, cols, 1),
        ),
        "blk",
        0,
    )
    grad_rot = lax.dynamic_slice_in_dim(grad_term, own_start, cols, 1) + grad_other
    moment_rot = lax.dynamic_slice_in_dim(moment_term, own_start, cols, 1) + moment_other
    variance = (
        variance_decay * exp_avg_sq.reshape(blocks * brows, cols)
        + (1.0 - variance_decay) * grad_rot * grad_rot
    )
    direction = (moment_rot / (jnp.sqrt(variance) + epsilon_value)).astype(jnp.bfloat16)
    partner_dir = from_partner(direction, "blk", 0)
    own_rows = lax.dynamic_slice_in_dim(right_rows, own_start, cols, 1)
    other_rows = lax.dynamic_slice_in_dim(right_rows, other_start, cols, 1)
    contract = (((1,), (1,)), ((), ()))
    back = lax.dot_general(direction, own_rows, contract, preferred_element_type=jnp.float32)
    back = back + lax.dot_general(
        partner_dir, other_rows, contract, preferred_element_type=jnp.float32
    )
    back = back.astype(jnp.bfloat16).reshape(blocks, brows, cols)
    back_group = lax.all_to_all(
        spread_block(back, groups), "row", split_axis=0, concat_axis=1, tiled=True
    )
    result = jnp.einsum(
        "nk,kc->nc", own_block, back_group[0], preferred_element_type=jnp.float32
    ).astype(jnp.bfloat16)
    update = join_block(
        lax.all_to_all(result[None], "row", split_axis=1, concat_axis=0, tiled=True), blocks, groups
    )
    return (update, moment, variance.reshape(blocks, brows, cols))


def solution(mesh):
    in_specs = (
        P(None, "row", "blk"),
        P(None, "row", "blk"),
        P(None, "row", "blk"),
        P(None, "row", "blk"),
        P("blk", "row"),
    )
    out_specs = (P(None, "row", "blk"), P(None, "row", "blk"), P(None, "row", "blk"))
    return jax.shard_map(body, mesh=mesh, in_specs=in_specs, out_specs=out_specs, check_vma=False)
```

profile of v0, /device:TPU:0, one launch (start us, length us, event | category | flops | bytes accessed | tf_op | source)
XLA Modules:
  0.0 226.6 jit_solution(1105288853827036145)
XLA Ops:
  8.7 20.0 %all_to_all.62 = bf16[4,256,512]{2,1,0:T(8,128)(2,1)} all-to-all(bf16[4,256,512]{2,1,0:T(8,128)(2,1)} %param.5), channel_id=1, replica_groups=mesh['row'=4,'blk'=8] {'row'}, dimensions={0} | all-to-all | bytes 2097152 | tf_op jit(solution)/shard_map/all_to_all | solution.py:44
  28.7 15.3 %all-gather.3.cloned.1.call-done = bf16[4,256,1024]{2,1,0:T(8,128)(2,1)} async-done(((bf16[4,256,128]{2,1,0:T(8,128)(2,1)}), bf16[4,256,1024]{2,1,0:T(8,128)(2,1)}) %all-gather.3.cloned.1.call-update) | async-done | bytes 2097168 | tf_op jit(solution)/shard_map/all_gather | solution.py:40
  44.0 4.5 %all-to-all-start.1 = ((bf16[4,256,1024]{2,1,0:T(8,128)(2,1)}), bf16[4,256,1024]{2,1,0:T(8,128)(2,1)}, u32[]{:S(2)}, u32[]{:S(2)}) async-start(bf16[4,256,1024]{2,1,0:T(8,128)(2,1)} %all-gather.3.cloned.1.call-done), calls=%async_computation.1 | async-start | bytes 4194304 | tf_op jit(solution)/shard_map/all_to_all | solution.py:50
  49.0 2.9 %copy.20 = f32[4,256,512]{1,2,0:T(8,128)} copy(f32[4,256,512]{2,1,0:T(8,128)} %param.6) | data formatting | bytes 4194304 | tf_op args[1]
  51.9 2.9 %fusion.16 = (bf16[4,256,512]{1,2,0:T(8,128)(2,1)}, f32[4,256,512]{1,2,0:T(8,128)S(1)}) fusion(bf16[4,256,512]{1,2,0:T(8,128)(2,1)S(1)} %copy.21, f32[4,256,512]{1,2,0:T(8,128)} %copy.20), kind=kLoop, calls=%fused_computation.25 | loop fusion | flops 2621440 | bytes 6291456 | tf_op jit(solution)/shard_map/convert_element_type | solution.py:39
  54.8 19.3 %all-to-all-done.1 = bf16[4,256,1024]{2,1,0:T(8,128)(2,1)} async-done(((bf16[4,256,1024]{2,1,0:T(8,128)(2,1)}), bf16[4,256,1024]{2,1,0:T(8,128)(2,1)}, u32[]{:S(2)}, u32[]{:S(2)}) %all-to-all-start.1) | async-done | bytes 2097184 | tf_op jit(solution)/shard_map/all_to_all | solution.py:50
  74.1 4.3 %all-to-all-start = ((bf16[4,256,512]{1,2,0:T(8,128)(2,1)}), bf16[4,256,512]{1,2,0:T(8,128)(2,1)}, u32[]{:S(2)}, u32[]{:S(2)}) async-start(bf16[4,256,512]{1,2,0:T(8,128)(2,1)} %get-tuple-element.14), calls=%async_computation | async-start | bytes 2097152 | tf_op jit(solution)/shard_map/all_to_all | solution.py:45
  79.0 2.9 %fusion.3 = bf16[1,1024,512]{2,1,0:T(8,128)(2,1)S(1)} fusion(bf16[4,256,1024]{2,1,0:T(8,128)(2,1)} %all-to-all-done.1, bf16[4,256,512]{2,1,0:T(8,128)(2,1)S(1)} %copy-done.5), kind=kOutput, calls=%fused_computation.10 | convolution fusion | flops 1074266112 | bytes 4194304 | tf_op jit(solution)/shard_map/kn,kc->nc/dot_general | solution.py:52
  81.8 2.9 %copy.40 = bf16[1,1024,512]{2,0,1:T(2,128)(2,1)} copy(bf16[1,1024,512]{2,1,0:T(8,128)(2,1)S(1)} %fusion.3) | data formatting | bytes 2097152 | tf_op jit(solution)/shard_map/broadcast_in_dim | solution.py:59
  85.4 8.1 %reduce.1 = bf16[1024,512]{1,0:T(8,128)(2,1)S(1)} reduce(bf16[1024,1,512]{2,1,0:T(2,128)(2,1)} %bitcast.51, bf16[]{:T(256)} %broadcast.3), dimensions={1}, to_apply=%bitcast.49.reduce_sub_computation | reduce | bytes 2097154
  95.5 4.1 %all-to-all-start.4 = ((bf16[4,2,65536]{2,1,0:T(2,128)(2,1)}), bf16[4,2,65536]{2,1,0:T(2,128)(2,1)S(1)}, u32[]{:S(2)}, u32[]{:S(2)}) async-start(bf16[4,2,65536]{2,1,0:T(2,128)(2,1)} %reshape.42), calls=%async_computation.4 | async-start | bytes 2097152 | tf_op jit(solution)/shard_map/all_to_all | solution.py:59
  99.6 4.3 %fusion.2 = bf16[1,1024,512]{1,2,0:T(8,128)(2,1)} fusion(bf16[4,256,512]{1,2,0:T(8,128)(2,1)} %all-to-all-done, bf16[4,256,1024]{2,1,0:T(8,128)(2,1)} %all-to-all-done.1), kind=kOutput, calls=%fused_computation.9 | convolution fusion | flops 1074266112 | bytes 4194304 | tf_op jit(solution)/shard_map/kn,kc->nc/dot_general | solution.py:55
  103.8 6.0 %copy.22 = bf16[1,1024,512]{2,0,1:T(2,128)(2,1)} copy(bf16[1,1024,512]{1,2,0:T(8,128)(2,1)} %fusion.2) | data formatting | bytes 2097152 | tf_op jit(solution)/shard_map/broadcast_in_dim | solution.py:60
  109.8 9.0 %reduce = bf16[1024,512]{1,0:T(8,128)(2,1)} reduce(bf16[1024,1,512]{2,1,0:T(2,128)(2,1)} %bitcast.53, bf16[]{:T(256)} %broadcast.3), dimensions={1}, to_apply=%bitcast.33.reduce_sub_computation | reduce | bytes 2097154
  118.8 3.7 %reshape.44 = bf16[4,2,65536]{2,1,0:T(2,128)(2,1)} reshape(bf16[1024,512]{1,0:T(8,128)(2,1)} %reduce) | data formatting | bytes 2097152
  122.6 4.3 %all-to-all-start.2 = ((bf16[4,2,65536]{2,1,0:T(2,128)(2,1)}), bf16[4,2,65536]{2,1,0:T(2,128)(2,1)}, u32[]{:S(2)}, u32[]{:S(2)}) async-start(bf16[4,2,65536]{2,1,0:T(2,128)(2,1)} %reshape.44), calls=%async_computation.2 | async-start | bytes 2097152 | tf_op jit(solution)/shard_map/all_to_all | solution.py:60
  126.9 2.3 %reshape.43 = bf16[1024,1,512]{2,1,0:T(2,128)(2,1)} reshape(bf16[4,2,65536]{2,1,0:T(2,128)(2,1)S(1)} %all-to-all-done.4) | data formatting | bytes 2097152
  129.2 3.1 %fusion.4 = f32[1024,1024]{1,0:T(8,128)S(1)} fusion(bf16[512,1024]{1,0:T(8,128)(2,1)} %all-gather.5.cloned.1.call-done, bf16[1,1024,512]{2,0,1:T(2,128)(2,1)} %bitcast.55), kind=kOutput, calls=%fused_computation.11 | convolution fusion | flops 1073741824 | bytes 6291456 | tf_op jit(solution)/shard_map/dot_general | solution.py:65
  135.8 4.1 %all-to-all-done.2 = bf16[4,2,65536]{2,1,0:T(2,128)(2,1)} async-done(((bf16[4,2,65536]{2,1,0:T(2,128)(2,1)}), bf16[4,2,65536]{2,1,0:T(2,128)(2,1)}, u32[]{:S(2)}, u32[]{:S(2)}) %all-to-all-start.2) | async-done | bytes 1048608 | tf_op jit(solution)/shard_map/all_to_all | solution.py:60
  139.9 4.0 %reshape.45 = bf16[1024,1,512]{2,1,0:T(2,128)(2,1)} reshape(bf16[4,2,65536]{2,1,0:T(2,128)(2,1)} %all-to-all-done.2) | data formatting | bytes 2097152
  143.9 2.8 %fusion.7 = f32[1024,1024]{1,0:T(8,128)S(1)} fusion(bf16[512,1024]{1,0:T(8,128)(2,1)S(1)} %copy-done.4, bf16[1,1024,512]{2,0,1:T(2,128)(2,1)} %bitcast.56), kind=kOutput, calls=%fused_computation.14 | convolution fusion | flops 1073741824 | bytes 6291456 | tf_op jit(solution)/shard_map/dot_general | solution.py:68
  149.9 2.0 broadcast_multiply_fusion
  153.8 3.0 %collective-permute-done.1 = f32[1024,512]{1,0:T(8,128)} collective-permute-done((f32[1024,512]{1,0:T(8,128)}, f32[1024,512]{1,0:T(8,128)}, u32[]{:S(2)}, u32[]{:S(2)}) %collective-permute-start.1) | collective-permute-done | bytes 2097184 | tf_op jit(solution)/shard_map/ppermute | solution.py:14
  156.8 5.5 %divide_convert_fusion = (bf16[1024,512]{1,0:T(8,128)(2,1)S(1)}, f32[1024,512]{1,0:T(8,128)}) fusion(f32[1024,512]{1,0:T(8,128)} %collective-permute-done, f32[1024,1024]{1,0:T(8,128)} %copy-done.3, s32[]{:T(128)S(6)} %select_n.18, f32[1024,512]{1,0:T(8,128)} %collective-permute-done.1, f32[1024,1024]{1,0:T(8,128)S(1)} %copy-done.2, ...), kind=kLoop, calls=%fused_computation.5 | loop fusion | flops 4194304 | bytes 13631492 | tf_op jit(solution)/shard_map/convert_element_type | solution.py:87
  162.4 2.5 %collective-permute-done.2 = bf16[1024,512]{1,0:T(8,128)(2,1)S(1)} collective-permute-done((bf16[1024,512]{1,0:T(8,128)(2,1)S(1)}, bf16[1024,512]{1,0:T(8,128)(2,1)S(1)}, u32[]{:S(2)}, u32[]{:S(2)}) %collective-permute-start.2) | collective-permute-done | bytes 1048608 | tf_op jit(solution)/shard_map/ppermute | solution.py:14
  166.5 17.1 %all_to_all.63 = bf16[4,256,512]{2,1,0:T(8,128)(2,1)S(1)} all-to-all(bf16[4,256,512]{2,1,0:T(8,128)(2,1)S(1)} %bitcast.54), channel_id=1, replica_groups=mesh['row'=4,'blk'=8] {'row'}, dimensions={0} | all-to-all | bytes 2097152 | tf_op jit(solution)/shard_map/all_to_all | solution.py:97
  183.6 2.9 %fusion.1 = bf16[1,1024,512]{1,2,0:T(8,128)(2,1)S(1)} fusion(bf16[1024,512]{1,0:T(8,128)(2,1)S(1)} %bitcast.59, bf16[1024,1024]{1,0:T(8,128)(2,1)} %bitcast.8), kind=kOutput, calls=%fused_computation.8 | convolution fusion | flops 1074266112 | bytes 4194304 | tf_op jit(solution)/shard_map/nk,kc->nc/dot_general | solution.py:100
  186.5 3.9 %copy.25 = bf16[1,1024,512]{2,0,1:T(2,128)(2,1)} copy(bf16[1,1024,512]{1,2,0:T(8,128)(2,1)S(1)} %fusion.1) | data formatting | bytes 2097152 | tf_op jit(solution)/shard_map/broadcast_in_dim | solution.py:104
  190.4 8.1 %reduce.2 = bf16[1024,512]{1,0:T(8,128)(2,1)S(1)} reduce(bf16[1024,1,512]{2,1,0:T(2,128)(2,1)} %bitcast.52, bf16[]{:T(256)} %broadcast.3), dimensions={1}, to_apply=%bitcast.35.reduce_sub_computation | reduce | bytes 2097154
  198.5 2.0 reshape.46
  200.5 3.5 %all-to-all-start.6 = ((bf16[4,2,65536]{2,1,0:T(2,128)(2,1)}), bf16[4,2,65536]{2,1,0:T(2,128)(2,1)S(1)}, u32[]{:S(2)}, u32[]{:S(2)}) async-start(bf16[4,2,65536]{2,1,0:T(2,128)(2,1)} %reshape.46), calls=%async_computation.6 | async-start | bytes 2097152 | tf_op jit(solution)/shard_map/all_to_all | solution.py:104
  205.8 11.1 %all-to-all-done.6 = bf16[4,2,65536]{2,1,0:T(2,128)(2,1)S(1)} async-done(((bf16[4,2,65536]{2,1,0:T(2,128)(2,1)}), bf16[4,2,65536]{2,1,0:T(2,128)(2,1)S(1)}, u32[]{:S(2)}, u32[]{:S(2)}) %all-to-all-start.6) | async-done | bytes 1048608 | tf_op jit(solution)/shard_map/all_to_all | solution.py:104
  (33 shorter events, 18.6 us)
Async XLA Ops:
  8.0 36.0 %all-gather.3.cloned.1.call-start = ((), (), s32[]{:S(2)}) async-start(), calls=%async_computation.7 | async-start | bytes 2359296 | tf_op jit(solution)/shard_map/all_gather | solution.py:40
  28.7 19.8 %copy-start = (bf16[4,256,512]{2,1,0:T(8,128)(2,1)S(1)}, bf16[4,256,512]{2,1,0:T(8,128)(2,1)}, u32[]{:S(2)}) copy-start(bf16[4,256,512]{2,1,0:T(8,128)(2,1)} %param.5) | copy-start | bytes 3145732
  44.0 30.1 %all-to-all-start.1 = ((bf16[4,256,1024]{2,1,0:T(8,128)(2,1)}), bf16[4,256,1024]{2,1,0:T(8,128)(2,1)}, u32[]{:S(2)}, u32[]{:S(2)}) async-start(bf16[4,256,1024]{2,1,0:T(8,128)(2,1)} %all-gather.3.cloned.1.call-done), calls=%async_computation.1 | async-start | bytes 4194304 | tf_op jit(solution)/shard_map/all_to_all | solution.py:50
  54.8 24.1 %copy-start.5 = (bf16[4,256,512]{2,1,0:T(8,128)(2,1)S(1)}, bf16[4,256,512]{2,1,0:T(8,128)(2,1)}, u32[]{:S(2)}) copy-start(bf16[4,256,512]{2,1,0:T(8,128)(2,1)} %all_to_all.62) | copy-start | bytes 3145732
  74.1 21.3 %all-to-all-start = ((bf16[4,256,512]{1,2,0:T(8,128)(2,1)}), bf16[4,256,512]{1,2,0:T(8,128)(2,1)}, u32[]{:S(2)}, u32[]{:S(2)}) async-start(bf16[4,256,512]{1,2,0:T(8,128)(2,1)} %get-tuple-element.14), calls=%async_computation | async-start | bytes 2097152 | tf_op jit(solution)/shard_map/all_to_all | solution.py:45
  78.4 50.8 %all-gather.5.cloned.1.call-start = ((), (), s32[]{:S(2)}) async-start(), calls=%async_computation.8 | async-start | bytes 1310720 | tf_op jit(solution)/shard_map/all_gather | solution.py:41
  95.5 27.1 %all-to-all-start.4 = ((bf16[4,2,65536]{2,1,0:T(2,128)(2,1)}), bf16[4,2,65536]{2,1,0:T(2,128)(2,1)S(1)}, u32[]{:S(2)}, u32[]{:S(2)}) async-start(bf16[4,2,65536]{2,1,0:T(2,128)(2,1)} %reshape.42), calls=%async_computation.4 | async-start | bytes 2097152 | tf_op jit(solution)/shard_map/all_to_all | solution.py:59
  122.6 17.3 %all-to-all-start.2 = ((bf16[4,2,65536]{2,1,0:T(2,128)(2,1)}), bf16[4,2,65536]{2,1,0:T(2,128)(2,1)}, u32[]{:S(2)}, u32[]{:S(2)}) async-start(bf16[4,2,65536]{2,1,0:T(2,128)(2,1)} %reshape.44), calls=%async_computation.2 | async-start | bytes 2097152 | tf_op jit(solution)/shard_map/all_to_all | solution.py:60
  132.3 2.0 copy-start.1
  135.8 8.1 %copy-start.4 = (bf16[512,1024]{1,0:T(8,128)(2,1)S(1)}, bf16[512,1024]{1,0:T(8,128)(2,1)}, u32[]{:S(2)}) copy-start(bf16[512,1024]{1,0:T(8,128)(2,1)} %all-gather.5.cloned.1.call-done) | copy-start | bytes 3145732
  146.7 2.6 %copy-start.3 = (f32[1024,1024]{1,0:T(8,128)}, f32[1024,1024]{1,0:T(8,128)S(1)}, u32[]{:S(2)}) copy-start(f32[1024,1024]{1,0:T(8,128)S(1)} %fusion.7) | copy-start | bytes 12582916
  149.3 4.5 %collective-permute-start = (f32[1024,512]{1,0:T(8,128)}, f32[1024,512]{1,0:T(8,128)}, u32[]{:S(2)}, u32[]{:S(2)}) collective-permute-start(f32[1024,512]{1,0:T(8,128)} %constant_dynamic-slice_fusion.1), channel_id=1, source_target_pairs={{0,1},{1,0},{2,3},{3,2},{4,5},{5,4},{6,7},{7,6},{8,9},{9,8},{10,11... | collective-permute-start | bytes 6291464 | tf_op jit(solution)/shard_map/ppermute | solution.py:14
  149.3 7.5 %collective-permute-start.1 = (f32[1024,512]{1,0:T(8,128)}, f32[1024,512]{1,0:T(8,128)}, u32[]{:S(2)}, u32[]{:S(2)}) collective-permute-start(f32[1024,512]{1,0:T(8,128)} %constant_dynamic-slice_fusion), channel_id=1, source_target_pairs={{0,1},{1,0},{2,3},{3,2},{4,5},{5,4},{6,7},{7,6},{8,9},{9,8},{10,11... | collective-permute-start | bytes 6291464 | tf_op jit(solution)/shard_map/ppermute | solution.py:14
  149.9 7.0 %copy-start.2 = (f32[1024,1024]{1,0:T(8,128)S(1)}, f32[1024,1024]{1,0:T(8,128)}, u32[]{:S(2)}) copy-start(f32[1024,1024]{1,0:T(8,128)} %copy-done.1) | copy-start | bytes 12582916
  162.3 2.7 %collective-permute-start.2 = (bf16[1024,512]{1,0:T(8,128)(2,1)S(1)}, bf16[1024,512]{1,0:T(8,128)(2,1)S(1)}, u32[]{:S(2)}, u32[]{:S(2)}) collective-permute-start(bf16[1024,512]{1,0:T(8,128)(2,1)S(1)} %get-tuple-element.12), channel_id=1, source_target_pairs={{0,1},{1,0},{2,3},{3,2},{4,5},{5,4},{6,7},{7,6},{8,9},{9,8},{10,11... | collective-permute-start | bytes 3145736 | tf_op jit(solution)/shard_map/ppermute | solution.py:14
  200.5 16.4 %all-to-all-start.6 = ((bf16[4,2,65536]{2,1,0:T(2,128)(2,1)}), bf16[4,2,65536]{2,1,0:T(2,128)(2,1)S(1)}, u32[]{:S(2)}, u32[]{:S(2)}) async-start(bf16[4,2,65536]{2,1,0:T(2,128)(2,1)} %reshape.46), calls=%async_computation.6 | async-start | bytes 2097152 | tf_op jit(solution)/shard_map/all_to_all | solution.py:104
Sparse Core Ops, SparseCore 0:
  10.4 33.5 all-gather.2
Sparse Core Ops, SparseCore 1:
  80.7 37.6 all-gather.4
where the time goes:
time: 228 us; the launch traced here: 227 us
  waiting for transfers between devices  58.4 us (26%)
  local copies, waits for them, and re-layouts  40.9 us (18%)
  blocking collectives  37.1 us (16%)
  other arithmetic  35.6 us (16%)
  starting transfers between devices  21.4 us (9%)
  matrix products  17.5 us (8%)
  between operations  15.6 us (7%)
    unnamed x3, other arithmetic  25.2 us
    unnamed x23, local copies, waits for them, and re-layouts  24.9 us
    all_to_all x1, blocking collectives, body(): lax.all_to_all(spread_block(grad, groups), 'row', split_axis=0, concat_ax...  20 us
    all_to_all x1, waiting for transfers between devices, body(): lax.all_to_all(picked, 'row', split_axis=0, concat_axis=0, tiled=True)  19.3 us
    all_to_all x1, blocking collectives, body(): lax.all_to_all(spread_block(back, groups), 'row', split_axis=0, concat_ax...  17.1 us
    all_gather x1, waiting for transfers between devices, body(): left_rows = lax.all_gather(left_basis, 'blk', axis=2, tiled=True)  15.3 us
    all_to_all x1, waiting for transfers between devices, body(): lax.all_to_all(result[None], 'row', split_axis=1, concat_axis=0, tiled=True)  11.1 us
    ppermute x3, waiting for transfers between devices, from_partner(): return lax.ppermute(value, axis, pairs)  7.5 us
  transfers between devices with their start and end apart: 10, of which 7 were waited for; matrix products, arithmetic and copies ran while one was open for 25% of the time, Pallas kernels for 0%

commit v1 on v0

--- a/solution.py
+++ b/solution.py
@@ -1,6 +1,10 @@
+import functools
+
 import jax
 import jax.numpy as jnp
 from jax import lax
+from jax.experimental import pallas as pl
+from jax.experimental.pallas import tpu as pltpu
 from jax.sharding import PartitionSpec as P
 
 momentum_decay = 0.9
@@ -33,7 +37,7 @@
     )
 
 
-def body(grad, exp_avg, exp_avg_sq, left_basis, right_basis):
+def general_body(grad, exp_avg, exp_avg_sq, left_basis, right_basis):
     blocks, brows, cols = grad.shape
     moment = momentum_decay * exp_avg + (1.0 - momentum_decay) * grad.astype(jnp.float32)
     moment_half = moment.astype(jnp.bfloat16)
@@ -106,6 +110,342 @@
     return (update, moment, variance.reshape(blocks, brows, cols))
 
 
+def kernel(
+    nrow,
+    nblk,
+    grad,
+    exp_avg,
+    exp_avg_sq,
+    left,
+    right,
+    rot_out,
+    update_out,
+    grad_own,
+    avg_own,
+    sq_own,
+    moment_half,
+    sq_half,
+    gathered,
+    sq_all,
+    basis,
+    turn,
+    turn_other,
+    turned,
+    turned_other,
+    grad_rot,
+    moment_rot,
+    rot_half,
+    direction,
+    direction_other,
+    back,
+    update,
+    send_sems,
+    recv_sems,
+    local_sems,
+):
+    brows, cols = grad.shape[1], grad.shape[2]
+    width = left.shape[2]
+    narrow = right.shape[1]
+    row = lax.axis_index("row")
+    blk = lax.axis_index("blk")
+    core = lax.rem(blk, 2)
+    partner = blk + 1 - 2 * core
+    counter = [0, 0]
+
+    def at_row(step):
+        return lax.rem(row + step, nrow)
+
+    def at_blk(step):
+        return lax.rem(blk + 2 * step, nblk)
+
+    def rows_of(index):
+        return pl.ds(pl.multiple_of(index * brows, brows), brows)
+
+    def lanes_of(index):
+        return pl.ds(pl.multiple_of(index * width, width), width)
+
+    def remote(source, target, to_row, to_blk):
+        index = counter[0]
+        counter[0] += 1
+        copy = pltpu.make_async_remote_copy(
+            src_ref=source,
+            dst_ref=target,
+            send_sem=send_sems.at[index],
+            recv_sem=recv_sems.at[index],
+            device_id=(to_row, to_blk),
+            device_id_type=pl.DeviceIdType.MESH,
+        )
+        copy.start()
+        return copy
+
+    def local(source, target):
+        index = counter[1]
+        counter[1] += 1
+        copy = pltpu.make_async_copy(source, target, local_sems.at[index])
+        copy.start()
+        return copy
+
+    load_grad = local(grad, grad_own)
+    load_avg = local(exp_avg, avg_own)
+    load_left = local(left.at[row], basis.at[rows_of(row), lanes_of(blk)])
+    load_block = local(grad.at[row], gathered.at[rows_of(row), pl.ds(0, cols)])
+    load_sq = local(exp_avg_sq, sq_own)
+
+    def right_place(source_row):
+        slot = lax.rem(source_row // (nrow // 2) + core, 2)
+        start = lax.rem(source_row, nrow // 2) * narrow
+        return turn.at[slot, :, pl.ds(pl.multiple_of(start, narrow), narrow)]
+
+    load_right = local(right, right_place(row))
+
+    barrier = pltpu.get_barrier_semaphore()
+    peers = [(at_row(step), blk) for step in range(1, nrow)]
+    peers += [(row, at_blk(step)) for step in range(1, nblk // 2)]
+    peers += [(row, partner)]
+    for peer in peers:
+        pl.semaphore_signal(barrier, inc=1, device_id=peer, device_id_type=pl.DeviceIdType.MESH)
+    pl.semaphore_wait(barrier, len(peers))
+
+    sent = []
+    left_copies = [
+        remote(left.at[at_row(step)], basis.at[rows_of(row), lanes_of(blk)], at_row(step), blk)
+        for step in range(1, nrow)
+    ]
+    grad_copies = [
+        remote(
+            grad.at[at_row(step)], gathered.at[rows_of(row), pl.ds(0, cols)], at_row(step), blk
+        )
+        for step in range(1, nrow)
+    ]
+    load_grad.wait()
+    load_avg.wait()
+    moment_copies = []
+    for step in list(range(1, nrow)) + [0]:
+        index = at_row(step)
+        moment = momentum_decay * avg_own[index] + (1.0 - momentum_decay) * grad_own[
+            index
+        ].astype(jnp.float32)
+        if step == 0:
+            gathered[rows_of(row), cols:] = moment.astype(jnp.bfloat16)
+        else:
+            moment_half[index] = moment.astype(jnp.bfloat16)
+            moment_copies.append(
+                remote(
+                    moment_half.at[index],
+                    gathered.at[rows_of(row), pl.ds(cols, cols)],
+                    index,
+                    blk,
+                )
+            )
+    right_copies = [
+        remote(right, right_place(row), at_row(step), blk) for step in range(1, nrow)
+    ]
+
+    load_left.wait()
+    for copy in left_copies:
+        copy.wait_recv()
+    own_lanes = basis.at[:, lanes_of(blk)]
+    spread_copies = [
+        remote(own_lanes, own_lanes, row, at_blk(step)) for step in range(1, nblk // 2)
+    ]
+    share_copies = [remote(own_lanes, own_lanes, row, partner)]
+
+    load_sq.wait()
+    sq_copies = []
+    for step in list(range(1, nrow)) + [0]:
+        index = at_row(step)
+        value = sq_own[index].astype(jnp.bfloat16)
+        if step == 0:
+            sq_all[rows_of(row), :] = value
+        else:
+            sq_half[index] = value
+
+    for step in range(1, nblk // 2):
+        spread_copies[step - 1].wait_recv()
+        lanes = basis.at[:, lanes_of(at_blk(nblk // 2 - step))]
+        share_copies.append(remote(lanes, lanes, row, partner))
+
+    for step in range(1, nrow):
+        index = at_row(step)
+        sq_copies.append(remote(sq_half.at[index], sq_all.at[rows_of(row), :], index, blk))
+
+    load_right.wait()
+    for copy in right_copies:
+        copy.wait_recv()
+    turn_copy = remote(turn.at[1], turn_other, row, partner)
+
+    load_block.wait()
+    for copy in share_copies + grad_copies + moment_copies:
+        copy.wait_recv()
+
+    turned_copies = []
+    for index in range(nrow):
+        part = pl.ds(index * brows, brows)
+        turned[part, :] = lax.dot_general(
+            basis[:, part],
+            gathered[...],
+            (((0,), (0,)), ((), ())),
+            preferred_element_type=jnp.float32,
+        ).astype(jnp.bfloat16)
+        turned_copies.append(remote(turned.at[part, :], turned_other.at[part, :], row, partner))
+
+    turn_copy.wait_recv()
+    for copy in turned_copies:
+        copy.wait_recv()
+    rot_copies = []
+    order = list(range(1, nrow)) + [0]
+    for step in order:
+        index = at_row(step)
+        part = rows_of(index)
+        grad_term = jnp.dot(turned[part, :cols], turn[0], preferred_element_type=jnp.float32)
+        grad_term += jnp.dot(
+            turned_other[part, :cols], turn_other[...], preferred_element_type=jnp.float32
+        )
+        grad_rot[part, :] = grad_term
+        rot_half[part, :] = grad_term.astype(jnp.bfloat16)
+        if step == 0:
+            rot_local = local(rot_half.at[part, :], rot_out.at[row])
+        else:
+            rot_copies.append(remote(rot_half.at[part, :], rot_out.at[row], index, blk))
+    for step in order:
+        part = rows_of(at_row(step))
+        moment_term = jnp.dot(turned[part, cols:], turn[0], preferred_element_type=jnp.float32)
+        moment_term += jnp.dot(
+            turned_other[part, cols:], turn_other[...], preferred_element_type=jnp.float32
+        )
+        moment_rot[part, :] = moment_term
+
+    direction_copies = []
+    for step in range(nrow):
+        index = at_row(nrow - step)
+        part = rows_of(index)
+        if step:
+            sq_copies[step - 1].wait_recv()
+        rotated = grad_rot[part, :]
+        variance = (
+            variance_decay * sq_all[part, :].astype(jnp.float32)
+            + (1.0 - variance_decay) * rotated * rotated
+        )
+        direction[part, :] = (
+            moment_rot[part, :] / (jnp.sqrt(variance) + epsilon_value)
+        ).astype(jnp.bfloat16)
+        direction_copies.append(
+            remote(direction.at[part, :], direction_other.at[part, :], row, partner)
+        )
+
+    contract = (((1,), (1,)), ((), ()))
+    for step in range(nrow):
+        part = rows_of(at_row(nrow - step))
+        direction_copies[step].wait_recv()
+        term = lax.dot_general(
+            direction[part, :], turn[0], contract, preferred_element_type=jnp.float32
+        )
+        term += lax.dot_general(
+            direction_other[part, :], turn[1], contract, preferred_element_type=jnp.float32
+        )
+        back[part, :] = term.astype(jnp.bfloat16)
+
+    update_copies = []
+    for step in order:
+        index = at_row(step)
+        part = rows_of(index)
+        update[part, :] = jnp.dot(
+            basis[part, :], back[...], preferred_element_type=jnp.float32
+        ).astype(jnp.bfloat16)
+        if step == 0:
+            update_local = local(update.at[part, :], update_out.at[row])
+        else:
+            update_copies.append(remote(update.at[part, :], update_out.at[row], index, blk))
+
+    rot_local.wait()
+    update_local.wait()
+    for copy in rot_copies + update_copies:
+        copy.wait_recv()
+    for copy in (
+        left_copies
+        + grad_copies
+        + moment_copies
+        + right_copies
+        + spread_copies
+        + share_copies
+        + sq_copies
+        + [turn_copy]
+        + turned_copies
+        + rot_copies
+        + direction_copies
+        + update_copies
+    ):
+        copy.wait_send()
+
+
+def fast_body(grad, exp_avg, exp_avg_sq, left_basis, right_basis):
+    blocks, brows, cols = grad.shape
+    nrow, nblk = lax.axis_size("row"), lax.axis_size("blk")
+    size = nrow * brows
+    half, full = jnp.bfloat16, jnp.float32
+    vmem = pltpu.VMEM
+    remote_count = 7 * (nrow - 1) + 2 * (nblk // 2 - 1) + 2 + 2 * nrow
+    rot, update = pl.pallas_call(
+        functools.partial(kernel, nrow, nblk),
+        out_shape=[jax.ShapeDtypeStruct(grad.shape, half)] * 2,
+        in_specs=[pl.BlockSpec(memory_space=pl.ANY)] * 5,
+        out_specs=[pl.BlockSpec(memory_space=pl.ANY)] * 2,
+        scratch_shapes=[
+            vmem(grad.shape, half),
+            vmem(grad.shape, full),
+            vmem(grad.shape, full),
+            vmem(grad.shape, half),
+            vmem(grad.shape, half),
+            vmem((size, 2 * cols), half),
+            vmem((size, cols), half),
+            vmem((size, size), half),
+            vmem((2, cols, cols), half),
+            vmem((cols, cols), half),
+            vmem((size, 2 * cols), half),
+            vmem((size, 2 * cols), half),
+            vmem((size, cols), full),
+            vmem((size, cols), full),
+            vmem((size, cols), half),
+            vmem((size, cols), half),
+            vmem((size, cols), half),
+            vmem((size, cols), half),
+            vmem((size, cols), half),
+            pltpu.SemaphoreType.DMA((remote_count,)),
+            pltpu.SemaphoreType.DMA((remote_count,)),
+            pltpu.SemaphoreType.DMA((8,)),
+        ],
+        compiler_params=pltpu.CompilerParams(
+            collective_id=0, has_side_effects=True, vmem_limit_bytes=56 * 2**20
+        ),
+        cost_estimate=pl.CostEstimate(
+            flops=12 * size * size * cols, bytes_accessed=16 * size * cols, transcendentals=0
+        ),
+    )(grad, exp_avg, exp_avg_sq, left_basis, right_basis)
+    moment = momentum_decay * exp_avg + (1.0 - momentum_decay) * grad.astype(full)
+    rotated = rot.astype(full)
+    variance = variance_decay * exp_avg_sq + (1.0 - variance_decay) * rotated * rotated
+    return (update, moment, variance)
+
+
+def body(grad, exp_avg, exp_avg_sq, left_basis, right_basis):
+    blocks, brows, cols = grad.shape
+    nrow, nblk = lax.axis_size("row"), lax.axis_size("blk")
+    size = nrow * brows
+    fits = (
+        blocks == nrow
+        and nrow % 2 == 0
+        and nblk * left_basis.shape[2] == size
+        and size == 2 * cols
+        and left_basis.shape[2] % 128 == 0
+        and right_basis.shape[0] == cols
+        and right_basis.shape[1] * nrow == size
+        and right_basis.shape[1] % 128 == 0
+        and brows % 128 == 0
+    )
+    run = fast_body if fits else general_body
+    return run(grad, exp_avg, exp_avg_sq, left_basis, right_basis)
+
+
 def solution(mesh):
     in_specs = (
         P(None, "row", "blk"),

time: 228 us -> 84.7 us (0.37)
  Pallas kernels: 0 us -> 78.6 us
  waiting for transfers between devices: 58.4 us -> 0 us
  local copies, waits for them, and re-layouts: 40.9 us -> 0.99 us
  blocking collectives: 37.1 us -> 0 us
  other arithmetic: 35.6 us -> 4.26 us
  starting transfers between devices: 21.4 us -> 0 us
  matrix products: 17.5 us -> 0 us
  between operations: 15.6 us -> 0.7 us
    pallas_call x0 -> x1, Pallas kernels: none -> 78.6 us  [fast_body(): pl.pallas_call(functools.partial(kernel, nrow, nblk), out_shape=[jax.Shap...]
    all_to_all x2 -> x0, blocking collectives: 37.1 us -> none  [the longest x1 20 us: body(): lax.all_to_all(spread_block(grad, groups), 'row', split_axis=0, concat_ax...]
    all_to_all x5 -> x0, waiting for transfers between devices: 34.4 us -> none  [the longest x1 19.3 us: body(): lax.all_to_all(picked, 'row', split_axis=0, concat_axis=0, tiled=True)]
    unnamed x3 -> x0, other arithmetic: 25.2 us -> none
    unnamed x23 -> x9, local copies, waits for them, and re-layouts: 24.9 us -> 0.99 us
    all_to_all x5 -> x0, starting transfers between devices: 20.7 us -> none  [the longest x1 4.49 us: body(): lax.all_to_all(picked, 'row', split_axis=0, concat_axis=0, tiled=True)]
    dot_general x7 -> x0, matrix products: 17.5 us -> none  [the longest x1 4.25 us: body(): jnp.einsum('kn,kc->nc', own_block, moment_group[0], preferred_element_typ...]
    all_gather x2 -> x0, waiting for transfers between devices: 15.3 us -> none  [the longest x1 15.3 us: body(): left_rows = lax.all_gather(left_basis, 'blk', axis=2, tiled=True)]
  transfers between devices with their start and end apart: 10 -> 0, of which waited for: 7 -> 0; matrix products, arithmetic and copies ran while one was open for 25% -> 0% of each run, Pallas kernels for 0% -> 0%
where the time goes in v1:
time: 84.7 us; the launch traced here: 84.5 us
  Pallas kernels  78.6 us (93%)
  other arithmetic  4.26 us (5%)
  local copies, waits for them, and re-layouts  0.99 us (1%)
    pallas_call x1, Pallas kernels, fast_body(): pl.pallas_call(functools.partial(kernel, nrow, nblk), out_shape=[jax.Shap...  78.6 us
    add x1, other arithmetic, fast_body(): variance_decay * exp_avg_sq + (1.0 - variance_decay) * rotated * rotated  4.26 us

profile of v1, /device:TPU:0, one launch (start us, length us, event | category | flops | bytes accessed | tf_op | source)
XLA Modules:
  0.0 84.5 jit_solution(7442864209426762438)
XLA Ops:
  0.6 0.0 copy-start.1
  0.6 0.0 copy-start
  0.7 0.0 copy-start.2
  0.7 78.6 %shard_map.76 = (bf16[4,256,512]{2,1,0:T(8,128)(2,1)}, bf16[4,256,512]{2,1,0:T(8,128)(2,1)}) custom-call(bf16[4,256,512]{2,1,0:T(8,128)(2,1)} %grad.1, f32[4,256,512]{2,1,0:T(8,128)} %exp_avg.1, f32[4,256,512]{2,1,0:T(8,128)} %exp_avg_sq.1, bf16[4,256,128]{2,1,0:T(8,128)(2,1)} %left.1, bf16[512,256]{1,0:T(8,128)(2,1)} %right.1), custom_call_target="tpu_custom_call" | custom-call | flops 6442450944 | bytes 8388608 | tf_op jit(solution)/shard_map/pallas_call | solution.py:388
  79.3 0.0 copy-done.1
  79.3 0.0 copy-done
  79.3 0.0 copy-done.2
  79.3 0.0 copy-start.3
  79.3 4.3 %fusion = (f32[4,256,512]{2,1,0:T(8,128)}, f32[4,256,512]{2,1,0:T(8,128)}) fusion(bf16[4,256,512]{2,1,0:T(8,128)(2,1)} %get-tuple-element.6, f32[4,256,512]{2,1,0:T(8,128)S(1)} %copy-done.1, bf16[4,256,512]{2,1,0:T(8,128)(2,1)S(1)} %copy-done.2, f32[4,256,512]{2,1,0:T(8,128)S(1)} %copy-done), kind=kLoop, calls=%fused_computation.1 | loop fusion | flops 4718592 | bytes 10485760 | tf_op jit(solution)/shard_map/add | solution.py:426
  83.6 0.0 copy-done.3
  83.6 1.0 %copy.9 = bf16[4,256,512]{2,1,0:T(8,128)(2,1)} copy(bf16[4,256,512]{2,1,0:T(8,128)(2,1)S(1)} %copy-done.3) | data formatting | bytes 2097152
Async XLA Ops:
  0.6 78.6 %copy-start.1 = (f32[4,256,512]{2,1,0:T(8,128)S(1)}, f32[4,256,512]{2,1,0:T(8,128)}, u32[]{:S(2)}) copy-start(f32[4,256,512]{2,1,0:T(8,128)} %exp_avg_sq.1) | copy-start | bytes 6291460
  0.6 78.6 %copy-start = (f32[4,256,512]{2,1,0:T(8,128)S(1)}, f32[4,256,512]{2,1,0:T(8,128)}, u32[]{:S(2)}) copy-start(f32[4,256,512]{2,1,0:T(8,128)} %exp_avg.1) | copy-start | bytes 6291460
  0.7 78.6 %copy-start.2 = (bf16[4,256,512]{2,1,0:T(8,128)(2,1)S(1)}, bf16[4,256,512]{2,1,0:T(8,128)(2,1)}, u32[]{:S(2)}) copy-start(bf16[4,256,512]{2,1,0:T(8,128)(2,1)} %grad.1) | copy-start | bytes 3145732
  79.3 4.3 %copy-start.3 = (bf16[4,256,512]{2,1,0:T(8,128)(2,1)S(1)}, bf16[4,256,512]{2,1,0:T(8,128)(2,1)}, u32[]{:S(2)}) copy-start(bf16[4,256,512]{2,1,0:T(8,128)(2,1)} %get-tuple-element.12) | copy-start | bytes 3145732

commit v2 on v1

--- a/solution.py
+++ b/solution.py
@@ -118,8 +118,10 @@
     exp_avg_sq,
     left,
     right,
+    update_out,
+    moment_out,
+    variance_out,
     rot_out,
-    update_out,
     grad_own,
     avg_own,
     sq_own,
@@ -206,52 +208,58 @@
         pl.semaphore_signal(barrier, inc=1, device_id=peer, device_id_type=pl.DeviceIdType.MESH)
     pl.semaphore_wait(barrier, len(peers))
 
-    sent = []
     left_copies = [
         remote(left.at[at_row(step)], basis.at[rows_of(row), lanes_of(blk)], at_row(step), blk)
         for step in range(1, nrow)
     ]
+    side, across = row + 1 - 2 * lax.rem(row, 2), lax.rem(row + 2, nrow)
+    right_copies = [remote(right, right_place(row), peer, blk) for peer in (side, across)]
     grad_copies = [
         remote(
             grad.at[at_row(step)], gathered.at[rows_of(row), pl.ds(0, cols)], at_row(step), blk
         )
         for step in range(1, nrow)
     ]
+    load_left.wait()
+    for copy in left_copies:
+        copy.wait_recv()
+    own_lanes = basis.at[:, lanes_of(blk)]
+    spread_copies = [
+        remote(own_lanes, own_lanes, row, at_blk(step)) for step in range(1, nblk // 2)
+    ]
+    share_copies = [remote(own_lanes, own_lanes, row, partner)]
+
     load_grad.wait()
     load_avg.wait()
-    moment_copies = []
     for step in list(range(1, nrow)) + [0]:
         index = at_row(step)
         moment = momentum_decay * avg_own[index] + (1.0 - momentum_decay) * grad_own[
             index
         ].astype(jnp.float32)
+        moment_out[index] = moment
         if step == 0:
             gathered[rows_of(row), cols:] = moment.astype(jnp.bfloat16)
         else:
             moment_half[index] = moment.astype(jnp.bfloat16)
-            moment_copies.append(
-                remote(
-                    moment_half.at[index],
-                    gathered.at[rows_of(row), pl.ds(cols, cols)],
-                    index,
-                    blk,
-                )
+
+    depth = cols // 2
+    right_copies[0].wait_recv()
+    first_half = right_place(side).at[pl.ds(0, depth)]
+    forward_copies = [remote(first_half, first_half, across, blk)]
+    right_copies[1].wait_recv()
+    second_half = right_place(across).at[pl.ds(depth, depth)]
+    forward_copies.append(remote(second_half, second_half, side, blk))
+
+    moment_copies = []
+    for step in range(1, nrow):
+        index = at_row(step)
+        moment_copies.append(
+            remote(
+                moment_half.at[index], gathered.at[rows_of(row), pl.ds(cols, cols)], index, blk
             )
-    right_copies = [
-        remote(right, right_place(row), at_row(step), blk) for step in range(1, nrow)
-    ]
-
-    load_left.wait()
-    for copy in left_copies:
-        copy.wait_recv()
-    own_lanes = basis.at[:, lanes_of(blk)]
-    spread_copies = [
-        remote(own_lanes, own_lanes, row, at_blk(step)) for step in range(1, nblk // 2)
-    ]
-    share_copies = [remote(own_lanes, own_lanes, row, partner)]
+        )
 
     load_sq.wait()
-    sq_copies = []
     for step in list(range(1, nrow)) + [0]:
         index = at_row(step)
         value = sq_own[index].astype(jnp.bfloat16)
@@ -260,67 +268,83 @@
         else:
             sq_half[index] = value
 
+    load_right.wait()
+    for copy in forward_copies:
+        copy.wait_recv()
+    turn_copy = remote(turn.at[1], turn_other, row, partner)
+
+    load_block.wait()
+    for copy in grad_copies:
+        copy.wait_recv()
+
+    sq_copies = []
+    for step in range(1, nrow):
+        index = at_row(step)
+        sq_copies.append(remote(sq_half.at[index], sq_all.at[rows_of(row), :], index, blk))
+
     for step in range(1, nblk // 2):
         spread_copies[step - 1].wait_recv()
         lanes = basis.at[:, lanes_of(at_blk(nblk // 2 - step))]
         share_copies.append(remote(lanes, lanes, row, partner))
-
-    for step in range(1, nrow):
-        index = at_row(step)
-        sq_copies.append(remote(sq_half.at[index], sq_all.at[rows_of(row), :], index, blk))
-
-    load_right.wait()
-    for copy in right_copies:
-        copy.wait_recv()
-    turn_copy = remote(turn.at[1], turn_other, row, partner)
-
-    load_block.wait()
-    for copy in share_copies + grad_copies + moment_copies:
-        copy.wait_recv()
-
-    turned_copies = []
-    for index in range(nrow):
-        part = pl.ds(index * brows, brows)
-        turned[part, :] = lax.dot_general(
-            basis[:, part],
-            gathered[...],
-            (((0,), (0,)), ((), ())),
-            preferred_element_type=jnp.float32,
-        ).astype(jnp.bfloat16)
-        turned_copies.append(remote(turned.at[part, :], turned_other.at[part, :], row, partner))
-
+    for copy in share_copies:
+        copy.wait_recv()
+
+    def turn_left(start):
+        copies = []
+        for index in range(nrow):
+            part = pl.ds(index * brows, brows)
+            place = (part, pl.ds(start, cols))
+            turned[place] = lax.dot_general(
+                basis[:, part],
+                gathered[:, pl.ds(start, cols)],
+                (((0,), (0,)), ((), ())),
+                preferred_element_type=jnp.float32,
+            ).astype(jnp.bfloat16)
+            copies.append(remote(turned.at[place], turned_other.at[place], row, partner))
+        return copies
+
+    def turn_right(part, start):
+        place = (part, pl.ds(start, cols))
+        term = jnp.dot(turned[place], turn[0], preferred_element_type=jnp.float32)
+        return term + jnp.dot(
+            turned_other[place], turn_other[...], preferred_element_type=jnp.float32
+        )
+
+    turned_copies = turn_left(0)
     turn_copy.wait_recv()
     for copy in turned_copies:
         copy.wait_recv()
-    rot_copies = []
     order = list(range(1, nrow)) + [0]
     for step in order:
-        index = at_row(step)
-        part = rows_of(index)
-        grad_term = jnp.dot(turned[part, :cols], turn[0], preferred_element_type=jnp.float32)
-        grad_term += jnp.dot(
-            turned_other[part, :cols], turn_other[...], preferred_element_type=jnp.float32
-        )
+        part = rows_of(at_row(step))
+        grad_term = turn_right(part, 0)
         grad_rot[part, :] = grad_term
         rot_half[part, :] = grad_term.astype(jnp.bfloat16)
-        if step == 0:
-            rot_local = local(rot_half.at[part, :], rot_out.at[row])
-        else:
-            rot_copies.append(remote(rot_half.at[part, :], rot_out.at[row], index, blk))
+    rot_local = local(rot_half.at[rows_of(row), :], rot_out.at[row])
+
+    for copy in moment_copies:
+        copy.wait_recv()
+    later_copies = turn_left(cols)
+    for copy in later_copies:
+        copy.wait_recv()
     for step in order:
         part = rows_of(at_row(step))
-        moment_term = jnp.dot(turned[part, cols:], turn[0], preferred_element_type=jnp.float32)
-        moment_term += jnp.dot(
-            turned_other[part, cols:], turn_other[...], preferred_element_type=jnp.float32
-        )
-        moment_rot[part, :] = moment_term
+        moment_rot[part, :] = turn_right(part, cols)
+
+    rot_copies = []
+
+    def send_rot():
+        for step in range(1, nrow):
+            index = at_row(step)
+            rot_copies.append(remote(rot_half.at[rows_of(index), :], rot_out.at[row], index, blk))
 
     direction_copies = []
     for step in range(nrow):
-        index = at_row(nrow - step)
-        part = rows_of(index)
+        part = rows_of(at_row(nrow - step))
         if step:
             sq_copies[step - 1].wait_recv()
+        if step == 1:
+            send_rot()
         rotated = grad_rot[part, :]
         variance = (
             variance_decay * sq_all[part, :].astype(jnp.float32)
@@ -358,19 +382,29 @@
             update_copies.append(remote(update.at[part, :], update_out.at[row], index, blk))
 
     rot_local.wait()
+    for step in range(nrow):
+        index = at_row(nrow - step)
+        if step:
+            rot_copies[step - 1].wait_recv()
+        rotated = rot_out[index].astype(jnp.float32)
+        variance_out[index] = (
+            variance_decay * sq_own[index] + (1.0 - variance_decay) * rotated * rotated
+        )
     update_local.wait()
-    for copy in rot_copies + update_copies:
+    for copy in update_copies:
         copy.wait_recv()
     for copy in (
         left_copies
         + grad_copies
         + moment_copies
         + right_copies
+        + forward_copies
         + spread_copies
         + share_copies
         + sq_copies
         + [turn_copy]
         + turned_copies
+        + later_copies
         + rot_copies
         + direction_copies
         + update_copies
@@ -384,13 +418,14 @@
     size = nrow * brows
     half, full = jnp.bfloat16, jnp.float32
     vmem = pltpu.VMEM
-    remote_count = 7 * (nrow - 1) + 2 * (nblk // 2 - 1) + 2 + 2 * nrow
-    rot, update = pl.pallas_call(
+    remote_count = 6 * (nrow - 1) + 4 + 2 * (nblk // 2 - 1) + 2 + 3 * nrow
+    return pl.pallas_call(
         functools.partial(kernel, nrow, nblk),
-        out_shape=[jax.ShapeDtypeStruct(grad.shape, half)] * 2,
+        out_shape=[vmem(grad.shape, half), vmem(grad.shape, full), vmem(grad.shape, full)],
         in_specs=[pl.BlockSpec(memory_space=pl.ANY)] * 5,
-        out_specs=[pl.BlockSpec(memory_space=pl.ANY)] * 2,
+        out_specs=[pl.BlockSpec(memory_space=vmem)] * 3,
         scratch_shapes=[
+            vmem(grad.shape, half),
             vmem(grad.shape, half),
             vmem(grad.shape, full),
             vmem(grad.shape, full),
@@ -421,11 +456,6 @@
             flops=12 * size * size * cols, bytes_accessed=16 * size * cols, transcendentals=0
         ),
     )(grad, exp_avg, exp_avg_sq, left_basis, right_basis)
-    moment = momentum_decay * exp_avg + (1.0 - momentum_decay) * grad.astype(full)
-    rotated = rot.astype(full)
-    variance = variance_decay * exp_avg_sq + (1.0 - variance_decay) * rotated * rotated
-    return (update, moment, variance)
-
 
 def body(grad, exp_avg, exp_avg_sq, left_basis, right_basis):
     blocks, brows, cols = grad.shape
@@ -433,7 +463,7 @@
     size = nrow * brows
     fits = (
         blocks == nrow
-        and nrow % 2 == 0
+        and nrow == 4
         and nblk * left_basis.shape[2] == size
         and size == 2 * cols
         and left_basis.shape[2] % 128 == 0

time: 84.7 us -> 80.2 us (0.947)
  other arithmetic: 4.26 us -> 0 us
  Pallas kernels: 78.6 us -> 75.8 us
  local copies, waits for them, and re-layouts: 0.99 us -> 3.61 us
    add x1 -> x0, other arithmetic: 4.26 us -> none  [fast_body(): variance_decay * exp_avg_sq + (1.0 - variance_decay) * rotated * rotated]
    pallas_call x1, Pallas kernels: 78.6 us -> 75.8 us  [fast_body(): pl.pallas_call(functools.partial(kernel, nrow, nblk), out_shape=[vmem(gra...]
    unnamed x9 -> x3, local copies, waits for them, and re-layouts: 0.99 us -> 3.61 us
where the time goes in v2:
time: 80.2 us; the launch traced here: 80 us
  Pallas kernels  75.8 us (95%)
  local copies, waits for them, and re-layouts  3.61 us (5%)
    pallas_call x1, Pallas kernels, fast_body(): pl.pallas_call(functools.partial(kernel, nrow, nblk), out_shape=[vmem(gra...  75.8 us
    unnamed x3, local copies, waits for them, and re-layouts  3.61 us

profile of v2, /device:TPU:0, one launch (start us, length us, event | category | flops | bytes accessed | tf_op | source)
XLA Modules:
  0.0 80.0 jit_solution(12971941220627219505)
XLA Ops:
  0.6 75.8 %shard_map.76 = (bf16[4,256,512]{2,1,0:T(8,128)(2,1)S(1)}, f32[4,256,512]{2,1,0:T(8,128)S(1)}, f32[4,256,512]{2,1,0:T(8,128)S(1)}) custom-call(bf16[4,256,512]{2,1,0:T(8,128)(2,1)} %grad.1, f32[4,256,512]{2,1,0:T(8,128)} %exp_avg.1, f32[4,256,512]{2,1,0:T(8,128)} %exp_avg_sq.1, bf16[4,256,128]{2,1,0:T(8,128)(2,1)} %left.1, bf16[512,256]{1,0:T(8,128)(2,1)} %right.1), custom_call_target="tpu_custom_call" | custom-call | flops 6442450944 | bytes 8388608 | tf_op jit(solution)/shard_map/pallas_call | solution.py:422
  76.4 1.0 %copy.11 = bf16[4,256,512]{2,1,0:T(8,128)(2,1)} copy(bf16[4,256,512]{2,1,0:T(8,128)(2,1)S(1)} %get-tuple-element.3) | data formatting | bytes 2097152
  77.4 1.3 %copy.12 = f32[4,256,512]{2,1,0:T(8,128)} copy(f32[4,256,512]{2,1,0:T(8,128)S(1)} %get-tuple-element.4) | data formatting | bytes 4194304
  78.7 1.3 %copy.13 = f32[4,256,512]{2,1,0:T(8,128)} copy(f32[4,256,512]{2,1,0:T(8,128)S(1)} %get-tuple-element.5) | data formatting | bytes 4194304
